TPU v7x, 256 devices: a whole 4x4x8 slice. The times are simulated.
256 devices in a mesh: row: 16 (over y, x), col: 8 (over z), feat: 2 (over core).
Axes of the slice: x: 4, y: 4, z: 8, core: 2. Of those that a mesh axis runs over, the one named last changes fastest.
Arguments:
- fresh: bfloat16 [65536, 512], P(('row', 'col'), 'feat'), may hold values from -6 to 6
- history: bfloat16 [65536, 512], P(('row', 'col'), 'feat'), may hold values from -6 to 6
- adj_val: bfloat16 [16, 8, 256, 128, 128], P('row', 'col'), may hold values from -0.0625 to 0.0625
- tile_row: int32 [16, 8, 256], P('row', 'col'), may hold values from 0 to 31
- tile_col: int32 [16, 8, 256], P('row', 'col'), may hold values from 0 to 63
- tile_count: int32 [16, 8], P('row', 'col'), may hold values from 64 to 256, as said below
- samp_id: int32 [16, 8, 48], P('row', 'col'), may hold values from 0 to 255, as said below
- samp_scale: float32 [16, 8, 48], P('row', 'col'), may hold values from 1 to 4
- weight: bfloat16 [512, 512], P('feat'), may hold values from -0.25 to 0.25
- d_out: bfloat16 [65536, 512], P(('row', 'col'), 'feat'), may hold values from -6 to 6
Outputs:
- layer_out: bfloat16 [65536, 512], P(('row', 'col'), 'feat')
- weight_grad: float32 [512, 512], P('feat')
- fresh_grad: float32 [65536, 512], P(('row', 'col'), 'feat')
Inputs may be any that keep to these rules, and one draw needn't show every extreme that they name: `tile_count`: at least a quarter of 256; some device has exactly 256; slots from this count on are ignored. `samp_id`: each is below its own device's tile_count; the largest slot and the first slot are each sampled somewhere.
All inputs are finite; a program needn't handle non-finite values.
Results may differ from a plain program's by a relative error of at most 0.015.
Values may be sent and summed in bfloat16 or wider, within the bound.
No kernel may reach another device: no remote copies, remote signals or barrier semaphores. Data moves between devices by JAX's collectives and lax.ppermute only.
A program may use at most 128 MiB of HBM per device.

v0:
```python
import jax
import jax.numpy as jnp
from jax import lax
from jax.sharding import PartitionSpec as P


def gelu_tanh(value):
    return jax.nn.gelu(value, approximate=True)


def local(
    fresh, history, adj_val, tile_row, tile_col, tile_count, samp_id, samp_scale, weight, d_out
):
    values = adj_val[0, 0]
    rows = tile_row[0, 0]
    cols = tile_col[0, 0]
    count = tile_count[0, 0]
    chosen = samp_id[0, 0]
    scales = samp_scale[0, 0]
    blk = values.shape[-1]
    half = fresh.shape[1]
    local_rows = fresh.shape[0]
    row_blocks = local_rows * lax.axis_size("col") // blk
    col_blocks = local_rows * lax.axis_size("row") // blk
    group = 32
    diff = (fresh.astype(jnp.float32) - history.astype(jnp.float32)).astype(jnp.bfloat16)
    col_diff, col_hist = (
        lax.all_gather(diff, "row", axis=0, tiled=True),
        lax.all_gather(history, "row", axis=0, tiled=True),
    )
    hist_blocks = col_hist.reshape(col_blocks, blk, half)
    diff_blocks = col_diff.reshape(col_blocks, blk, half)

    def tile_step(step, total):
        start = step * group
        part_vals = lax.dynamic_slice_in_dim(values, start, group, 0)
        part_rows = lax.dynamic_slice_in_dim(rows, start, group, 0)
        part_cols = lax.dynamic_slice_in_dim(cols, start, group, 0)
        live = (start + jnp.arange(group, dtype=jnp.int32) < count).astype(jnp.float32)
        inputs = hist_blocks[part_cols]
        product = jnp.einsum("tij,tjd->tid", part_vals, inputs, preferred_element_type=jnp.float32)
        return total.at[part_rows].add(product * live[:, None, None])

    trips = values.shape[0] // group
    start_acc = jnp.zeros((row_blocks, blk, half), jnp.float32)
    total = lax.fori_loop(0, trips, tile_step, start_acc)
    sampled = values[chosen]
    samp_rows = rows[chosen]
    samp_cols = cols[chosen]
    sdiff = diff_blocks[samp_cols]
    sproduct = (
        jnp.einsum("tij,tjd->tid", sampled, sdiff, preferred_element_type=jnp.float32)
        * scales[:, None, None]
    )
    total = total.at[samp_rows].add(sproduct)
    zsum = lax.psum_scatter(
        total.reshape(row_blocks * blk, half), "col", scatter_dimension=0, tiled=True
    )
    zval = zsum.astype(jnp.bfloat16)
    partial_value = jnp.dot(zval, weight, preferred_element_type=jnp.float32)
    pre = lax.psum_scatter(partial_value, "feat", scatter_dimension=1, tiled=True)
    layer_out, pull = jax.vjp(gelu_tanh, pre)
    grad_pre = pull(d_out.astype(jnp.float32))[0].astype(jnp.bfloat16)
    grad_full = lax.all_gather(grad_pre, "feat", axis=1, tiled=True)
    weight_part = lax.dot_general(
        zval, grad_full, (((0,), (0,)), ((), ())), preferred_element_type=jnp.float32
    )
    weight_grad = lax.psum(weight_part, ("row", "col"))
    dz_val = lax.dot_general(
        grad_full, weight, (((1,), (1,)), ((), ())), preferred_element_type=jnp.float32
    ).astype(jnp.bfloat16)
    dz_rows = lax.all_gather(dz_val, "col", axis=0, tiled=True)
    dz_blocks = dz_rows.reshape(row_blocks, blk, half)
    grads = dz_blocks[samp_rows]
    bproduct = (
        jnp.einsum("tji,tjd->tid", sampled, grads, preferred_element_type=jnp.float32)
        * scales[:, None, None]
    )
    back = (
        jnp.zeros((col_blocks, blk, half), jnp.float32)
        .at[samp_cols]
        .add(bproduct)
        .reshape(col_blocks * blk, half)
    )
    fresh_grad = lax.psum_scatter(
        back.astype(jnp.bfloat16), "row", scatter_dimension=0, tiled=True
    ).astype(jnp.float32)
    return (layer_out.astype(jnp.bfloat16), weight_grad, fresh_grad)


def solution(mesh):
    placed = (
        P(("row", "col"), "feat"),
        P(("row", "col"), "feat"),
        P("row", "col", None, None, None),
        P("row", "col", None),
        P("row", "col", None),
        P("row", "col"),
        P("row", "col", None),
        P("row", "col", None),
        P("feat", None),
        P(("row", "col"), "feat"),
    )
    return jax.shard_map(
        local,
        mesh=mesh,
        in_specs=placed,
        out_specs=(P(("row", "col"), "feat"), P("feat", None), P(("row", "col"), "feat")),
        check_vma=False,
    )
```

profile of v0, /device:TPU:2, one launch (start us, length us, event | category | flops | bytes accessed | tf_op | source)
XLA Modules:
  0.0 702.2 jit_solution(11072576003868995876)
XLA Ops:
  7.2 0.7 all-gather.4.cloned.1.call-update
  8.0 1.8 subtract_convert_fusion
  9.8 0.7 fusion.16
  10.5 1.5 gather_fusion.1
  12.1 5.3 gather_fusion.2
  17.4 0.8 gather_fusion.3
  18.2 51.8 %all-gather.4.cloned.1.call-done = bf16[8192,256]{1,0:T(8,128)(2,1)} async-done(((bf16[512,256]{1,0:T(8,128)(2,1)}), bf16[8192,256]{1,0:T(8,128)(2,1)}) %all-gather.4.cloned.1.call-update) | async-done | bytes 4194320 | tf_op jit(solution)/shard_map/all_gather | solution.py:29
  70.0 2.4 broadcast_in_dim.30
  72.4 140.4 %while.13 = (s32[]{:T(128)}, f32[32,128,256]{2,1,0:T(8,128)}, s32[256]{0:T(256)S(1)}, bf16[256,128,128]{2,1,0:T(8,128)(2,1)}, s32[256]{0:T(256)S(1)}, /*index=5*...) while((s32[]{:T(128)}, f32[32,128,256]{2,1,0:T(8,128)}, ...), condition=%wide.region_2.0_spmd, body=%wide.region_0.0_spmd.sunk | while | flops 270533920 | bytes 24122676 | solution.py:46
  72.5 2.9 gather_fusion
  75.4 0.7 compare_convert_fusion.2
  76.0 3.9 convolution_multiply_fusion.2
  79.9 10.1 %scatter_fusion = f32[32,128,256]{2,1,0:T(8,128)} fusion(f32[32,128,256]{2,1,0:T(8,128)} %get-tuple-element.205, s32[32]{0:T(128)S(1)} %get-tuple-element.191, f32[32,128,256]{2,1,0:T(8,128)} %convolution_multiply_fusion.2), kind=kCustom, calls=%fused_computation.6.clone.1 | custom fusion | flops 1048576 | bytes 12583040 | tf_op jit(solution)/shard_map/while/body/eval_jaxpr/scatter-add | solution.py:42
  90.1 0.1 compare_select_fusion.6
  90.2 2.9 gather_fusion
  93.1 0.7 compare_convert_fusion.2
  93.8 3.9 convolution_multiply_fusion.2
  97.7 9.8 %scatter_fusion = f32[32,128,256]{2,1,0:T(8,128)} fusion(f32[32,128,256]{2,1,0:T(8,128)} %get-tuple-element.205, s32[32]{0:T(128)S(1)} %get-tuple-element.191, f32[32,128,256]{2,1,0:T(8,128)} %convolution_multiply_fusion.2), kind=kCustom, calls=%fused_computation.6.clone.1 | custom fusion | flops 1048576 | bytes 12583040 | tf_op jit(solution)/shard_map/while/body/eval_jaxpr/scatter-add | solution.py:42
  107.5 0.1 compare_select_fusion.6
  107.6 3.2 gather_fusion
  110.8 0.7 compare_convert_fusion.2
  111.5 3.9 convolution_multiply_fusion.2
  115.4 10.1 %scatter_fusion = f32[32,128,256]{2,1,0:T(8,128)} fusion(f32[32,128,256]{2,1,0:T(8,128)} %get-tuple-element.205, s32[32]{0:T(128)S(1)} %get-tuple-element.191, f32[32,128,256]{2,1,0:T(8,128)} %convolution_multiply_fusion.2), kind=kCustom, calls=%fused_computation.6.clone.1 | custom fusion | flops 1048576 | bytes 12583040 | tf_op jit(solution)/shard_map/while/body/eval_jaxpr/scatter-add | solution.py:42
  125.6 2.9 gather_fusion
  128.5 0.7 compare_convert_fusion.2
  129.1 3.9 convolution_multiply_fusion.2
  133.1 10.0 %scatter_fusion = f32[32,128,256]{2,1,0:T(8,128)} fusion(f32[32,128,256]{2,1,0:T(8,128)} %get-tuple-element.205, s32[32]{0:T(128)S(1)} %get-tuple-element.191, f32[32,128,256]{2,1,0:T(8,128)} %convolution_multiply_fusion.2), kind=kCustom, calls=%fused_computation.6.clone.1 | custom fusion | flops 1048576 | bytes 12583040 | tf_op jit(solution)/shard_map/while/body/eval_jaxpr/scatter-add | solution.py:42
  143.2 2.9 gather_fusion
  146.0 0.7 compare_convert_fusion.2
  146.7 3.9 convolution_multiply_fusion.2
  150.6 9.9 %scatter_fusion = f32[32,128,256]{2,1,0:T(8,128)} fusion(f32[32,128,256]{2,1,0:T(8,128)} %get-tuple-element.205, s32[32]{0:T(128)S(1)} %get-tuple-element.191, f32[32,128,256]{2,1,0:T(8,128)} %convolution_multiply_fusion.2), kind=kCustom, calls=%fused_computation.6.clone.1 | custom fusion | flops 1048576 | bytes 12583040 | tf_op jit(solution)/shard_map/while/body/eval_jaxpr/scatter-add | solution.py:42
  160.6 2.9 gather_fusion
  163.5 0.7 compare_convert_fusion.2
  164.1 3.9 convolution_multiply_fusion.2
  168.0 10.0 %scatter_fusion = f32[32,128,256]{2,1,0:T(8,128)} fusion(f32[32,128,256]{2,1,0:T(8,128)} %get-tuple-element.205, s32[32]{0:T(128)S(1)} %get-tuple-element.191, f32[32,128,256]{2,1,0:T(8,128)} %convolution_multiply_fusion.2), kind=kCustom, calls=%fused_computation.6.clone.1 | custom fusion | flops 1048576 | bytes 12583040 | tf_op jit(solution)/shard_map/while/body/eval_jaxpr/scatter-add | solution.py:42
  178.1 2.9 gather_fusion
  181.0 0.7 compare_convert_fusion.2
  181.6 3.9 convolution_multiply_fusion.2
  185.5 9.9 %scatter_fusion = f32[32,128,256]{2,1,0:T(8,128)} fusion(f32[32,128,256]{2,1,0:T(8,128)} %get-tuple-element.205, s32[32]{0:T(128)S(1)} %get-tuple-element.191, f32[32,128,256]{2,1,0:T(8,128)} %convolution_multiply_fusion.2), kind=kCustom, calls=%fused_computation.6.clone.1 | custom fusion | flops 1048576 | bytes 12583040 | tf_op jit(solution)/shard_map/while/body/eval_jaxpr/scatter-add | solution.py:42
  195.5 2.9 gather_fusion
  198.4 0.7 compare_convert_fusion.2
  199.1 3.9 convolution_multiply_fusion.2
  203.0 9.9 %scatter_fusion = f32[32,128,256]{2,1,0:T(8,128)} fusion(f32[32,128,256]{2,1,0:T(8,128)} %get-tuple-element.205, s32[32]{0:T(128)S(1)} %get-tuple-element.191, f32[32,128,256]{2,1,0:T(8,128)} %convolution_multiply_fusion.2), kind=kCustom, calls=%fused_computation.6.clone.1 | custom fusion | flops 1048576 | bytes 12583040 | tf_op jit(solution)/shard_map/while/body/eval_jaxpr/scatter-add | solution.py:42
  212.8 4.9 gather_fusion.4
  217.7 5.5 broadcast_multiply_fusion.1
  223.2 14.6 %scatter_fusion.1 = f32[32,128,256]{2,1,0:T(8,128)} fusion(f32[32,128,256]{2,1,0:T(8,128)} %get-tuple-element.127, s32[48]{0:T(128)S(1)} %fusion.17, f32[48,128,256]{2,1,0:T(8,128)} %broadcast_multiply_fusion.1), kind=kCustom, calls=%fused_computation.7 | custom fusion | flops 1572864 | bytes 18874560 | tf_op jit(solution)/shard_map/scatter-add | solution.py:55
  238.0 54.7 %reduce-scatter.4.cloned.1.call-done = f32[512,256]{1,0:T(8,128)} async-done(((f32[4096,256]{1,0:T(8,128)}), f32[512,256]{1,0:T(8,128)}) %reduce-scatter.4.cloned.1.call-update) | async-done | bytes 524304 | tf_op jit(solution)/shard_map/reduce_scatter | solution.py:56
  292.6 2.3 fusion.14
  295.0 12.6 %reduce-scatter.6.cloned.1.call-done = f32[512,256]{1,0:T(8,128)} async-done(((f32[512,512]{1,0:T(8,128)}), f32[512,256]{1,0:T(8,128)}) %reduce-scatter.6.cloned.1.call-update) | async-done | bytes 524304 | tf_op jit(solution)/shard_map/reduce_scatter | solution.py:61
  307.6 2.1 fusion.4
  309.8 2.2 all_gather.14
  311.9 1.0 convolution_convert_fusion
  313.1 42.5 %all-gather.8.cloned.1.call-done = bf16[4096,256]{1,0:T(8,128)(2,1)} async-done(((bf16[512,256]{1,0:T(8,128)(2,1)}), bf16[4096,256]{1,0:T(8,128)(2,1)}) %all-gather.8.cloned.1.call-update) | async-done | bytes 2097168 | tf_op jit(solution)/shard_map/all_gather | solution.py:72
  355.6 4.1 gather_fusion.5
  359.7 5.8 broadcast_multiply_fusion
  365.5 4.3 broadcast_in_dim.31
  369.7 14.7 %scatter_fusion.2 = f32[64,128,256]{2,1,0:T(8,128)} fusion(f32[64,128,256]{2,1,0:T(8,128)} %broadcast_in_dim.31, s32[48]{0:T(128)S(1)} %fusion.18, f32[48,128,256]{2,1,0:T(8,128)} %broadcast_multiply_fusion), kind=kCustom, calls=%fused_computation.8 | custom fusion | flops 1572864 | bytes 18874560 | tf_op jit(solution)/shard_map/scatter-add | solution.py:82
  384.4 6.0 convert_element_type.52
  390.4 1.0 copy-done.4
  391.4 1.1 fusion.12
  392.5 78.8 %reduce-scatter.8.cloned.1.call-done = bf16[512,256]{1,0:T(8,128)(2,1)} async-done(((bf16[8192,256]{1,0:T(8,128)(2,1)}), bf16[512,256]{1,0:T(8,128)(2,1)}) %reduce-scatter.8.cloned.1.call-update) | async-done | bytes 262160 | tf_op jit(solution)/shard_map/reduce_scatter | solution.py:85
  471.4 1.8 convert_element_type.54
  473.2 220.3 %all-reduce.2.cloned.1.call-done = f32[256,512]{1,0:T(8,128)} async-done(((f32[256,512]{1,0:T(8,128)}), f32[256,512]{1,0:T(8,128)}) %all-reduce.2.cloned.1.call-update) | async-done | bytes 524304 | tf_op jit(solution)/shard_map/psum | solution.py:68
  693.5 1.9 copy.26
  (46 shorter events, 1.0 us)
Async XLA Ops:
  7.2 285.5 %copy-start = (bf16[256,512]{1,0:T(8,128)(2,1)S(1)}, bf16[256,512]{1,0:T(8,128)(2,1)}, u32[]{:S(2)}) copy-start(bf16[256,512]{1,0:T(8,128)(2,1)} %param.20) | copy-start | bytes 786436
  7.2 10.2 %copy-start.2 = (s32[1,1,256]{2,1,0:T(1,128)S(1)}, s32[1,1,256]{2,1,0:T(1,128)}, u32[]{:S(2)}) copy-start(s32[1,1,256]{2,1,0:T(1,128)} %param.16) | copy-start | bytes 3076
  7.2 62.8 %all-gather.4.cloned.1.call-start = ((), (), s32[]{:S(2)}) async-start(), calls=%async_computation.3 | async-start | bytes 4456448 | tf_op jit(solution)/shard_map/all_gather | solution.py:29
  7.9 204.9 %all-gather.6.cloned.1.call-start = ((), (), s32[]{:S(2)}) async-start(), calls=%async_computation.4 | async-start | bytes 4456448 | tf_op jit(solution)/shard_map/all_gather | solution.py:28
  9.8 282.8 %reduce-scatter.4.cloned.1.call-start = ((), (), s32[]{:S(2)}) async-start(), calls=%async_computation.5 | async-start | bytes 4718592 | tf_op jit(solution)/shard_map/reduce_scatter | solution.py:56
  10.5 61.9 %copy-start.1 = (s32[1,1,256]{2,1,0:T(1,128)S(1)}, s32[1,1,256]{2,1,0:T(1,128)}, u32[]{:S(2)}) copy-start(s32[1,1,256]{2,1,0:T(1,128)} %param.15) | copy-start | bytes 3076
  212.8 4.9 copy-start.3
  212.8 4.9 copy-start.6
  237.9 69.7 %copy-start.5 = (bf16[512,256]{1,0:T(8,128)(2,1)S(1)}, bf16[512,256]{1,0:T(8,128)(2,1)}, u32[]{:S(2)}) copy-start(bf16[512,256]{1,0:T(8,128)(2,1)} %param.21) | copy-start | bytes 786436
  237.9 69.7 %reduce-scatter.6.cloned.1.call-start = ((), (), s32[]{:S(2)}) async-start(), calls=%async_computation.6 | async-start | bytes 1572864 | tf_op jit(solution)/shard_map/reduce_scatter | solution.py:61
  295.0 60.6 %all-gather.8.cloned.1.call-start = ((), (), s32[]{:S(2)}) async-start(), calls=%async_computation.8 | async-start | bytes 2359296 | tf_op jit(solution)/shard_map/all_gather | solution.py:72
  313.0 158.4 %reduce-scatter.8.cloned.1.call-start = ((), (), s32[]{:S(2)}) async-start(), calls=%async_computation.9 | async-start | bytes 4456448 | tf_op jit(solution)/shard_map/reduce_scatter | solution.py:85
  390.3 1.0 copy-start.4
  390.4 303.1 %all-reduce.2.cloned.1.call-start = ((), (), s32[]{:S(2)}) async-start(), calls=%async_computation.7 | async-start | bytes 1048576 | tf_op jit(solution)/shard_map/psum | solution.py:68
Sparse Core Ops, SparseCore 0:
  10.5 59.4 all-gather.3
  73.0 56.2 all-gather.5
  238.0 54.5 reduce-scatter.3
  295.1 12.4 reduce-scatter.5
  313.1 42.4 all-gather.7
  390.5 80.8 reduce-scatter.7
  477.4 216.0 all-reduce.1
where the time goes:
time: 704 us; the launch traced here: 702 us
  waiting for transfers between devices  462 us (66%)
  other arithmetic  127 us (18%)
  local copies, waits for them, and re-layouts  49.5 us (7%)
  matrix products  47.1 us (7%)
  between operations  14.2 us (2%)
    psum x1, waiting for transfers between devices, local(): weight_grad = lax.psum(weight_part, ('row', 'col'))  220 us
    scatter-add x8, other arithmetic, tile_step(): return total.at[part_rows].add(product * live[:, None, None])  79.7 us
    reduce_scatter x1, waiting for transfers between devices, local(): lax.psum_scatter(back.astype(jnp.bfloat16), 'row', scatter_dimension=0, t...  78.8 us
    reduce_scatter x1, waiting for transfers between devices, local(): lax.psum_scatter(total.reshape(row_blocks * blk, half), 'col', scatter_di...  54.7 us
    all_gather x1, waiting for transfers between devices, local(): lax.all_gather(history, 'row', axis=0, tiled=True)  51.8 us
    all_gather x1, waiting for transfers between devices, local(): dz_rows = lax.all_gather(dz_val, 'col', axis=0, tiled=True)  42.5 us
    dot_general x8, matrix products, tile_step(): jnp.einsum('tij,tjd->tid', part_vals, inputs, preferred_element_type=jnp....  31.3 us
    gather x8, local copies, waits for them, and re-layouts, tile_step(): inputs = hist_blocks[part_cols]  23.4 us
  transfers between devices with their start and end apart: 7, of which 6 were waited for; matrix products, arithmetic and copies ran while one was open for 22% of the time, Pallas kernels for 0%

commit v1 on v0

v1 whole, which is shorter than its diff:
```python
import functools
import jax
import jax.numpy as jnp
from jax import lax
from jax.experimental import pallas as pl
from jax.experimental.pallas import tpu as pltpu
from jax.sharding import Mesh, PartitionSpec as P

BF = jnp.bfloat16
F32 = jnp.float32
GROUP = 8
CHUNKS = 8
VMEM = pl.BlockSpec(memory_space=pltpu.VMEM)
HBM = pl.BlockSpec(memory_space=pl.ANY)
SMEM = pl.BlockSpec(memory_space=pltpu.SMEM)


def shift(x, axis, step):
    n = lax.axis_size(axis)
    return lax.ppermute(x, axis, [(i, (i + step) % n) for i in range(n)])


def gather_two(x, first, second):
    group = jnp.concatenate(
        [x, shift(x, first, -1), shift(x, first, 2), shift(x, first, 1)], axis=0
    )
    below = shift(group, second, 1)
    above = shift(group, second, -1)
    half = group.shape[0] // 2
    far_lo = shift(below[:half], second, 1)
    far_hi = shift(above[half:], second, -1)
    return group, above, far_lo, far_hi, below


def gather_copies(parts, dst, sems, base):
    copies = []
    at = 0
    for n, part in enumerate(parts):
        size = part.shape[0]
        copies.append(pltpu.make_async_copy(part, dst.at[pl.ds(at, size)], sems.at[base + n]))
        at += size
    return copies


def forward_kernel(
    rows, cols, srow, scol, sid, meta, scale, adj,
    h0, h1, h2, h3, h4, d0, d1, d2, d3, d4,
    o4a, o4b, o3, o2, o1, o0, m1, m2, m3,
    tiles, hist, diff, acc, sems,
):
    count = meta[0]
    zpos = meta[1]
    nodes = gather_copies((h0, h1, h2, h3, h4), hist, sems, 0)
    nodes += gather_copies((d0, d1, d2, d3, d4), diff, sems, 5)
    per = tiles.shape[0] // CHUNKS
    loads = [
        pltpu.make_async_copy(
            adj.at[pl.ds(c * per, per)], tiles.at[pl.ds(c * per, per)], sems.at[10 + c]
        )
        for c in range(CHUNKS)
    ]
    for copy in nodes[:5]:
        copy.start()
    for copy in loads:
        copy.start()
    for copy in nodes[5:]:
        copy.start()
    acc[...] = jnp.zeros_like(acc)
    for copy in nodes[:5]:
        copy.wait()
    groups = (count + GROUP - 1) // GROUP
    each = per // GROUP

    for c in range(CHUNKS):
        loads[c].wait()

        def body(g, carry):
            start = g * GROUP
            products = [
                jnp.dot(tiles[start + u], hist[cols[start + u]], preferred_element_type=F32)
                for u in range(GROUP)
            ]
            for u in range(GROUP):
                r = rows[start + u]
                acc[r] = acc[r] + products[u]
            return carry

        lax.fori_loop(c * each, jnp.clip(groups, c * each, (c + 1) * each), body, 0)
    for copy in nodes[5:]:
        copy.wait()

    def sampled(g, carry):
        start = g * GROUP
        products = [
            jnp.dot(
                tiles[sid[start + u]], diff[scol[start + u]], preferred_element_type=F32
            )
            * scale[start + u]
            for u in range(GROUP)
        ]
        for u in range(GROUP):
            r = srow[start + u]
            acc[r] = acc[r] + products[u]
        return carry

    lax.fori_loop(0, sid.shape[0] // GROUP, sampled, 0)

    def put(out, k, lo, size):
        start = lax.rem(zpos + k, 8) * 4 + lo
        out[...] = acc[pl.ds(start, size)].astype(out.dtype)

    put(o4a, 4, 0, 2)
    put(o4b, 4, 2, 2)
    for out, k in ((o3, 3), (o2, 2), (o1, 1), (o0, 0), (m1, 7), (m2, 6), (m3, 5)):
        put(out, k, 0, 4)


def forward_tiles(rows, cols, srow, scol, sid, meta, scale, adj, hist, diff):
    n_tiles, blk, _ = adj.shape
    half = hist[0].shape[-1]
    whole = jax.ShapeDtypeStruct((4, blk, half), BF)
    part = jax.ShapeDtypeStruct((2, blk, half), BF)
    return pl.pallas_call(
        forward_kernel,
        out_shape=[part, part, whole, whole, whole, whole, whole, whole, whole],
        in_specs=[SMEM] * 7 + [HBM] * 11,
        out_specs=[VMEM] * 9,
        scratch_shapes=[
            pltpu.VMEM((n_tiles, blk, blk), BF),
            pltpu.VMEM((64, blk, half), BF),
            pltpu.VMEM((64, blk, half), BF),
            pltpu.VMEM((33, blk, half), F32),
            pltpu.SemaphoreType.DMA((10 + CHUNKS,)),
        ],
        compiler_params=pltpu.CompilerParams(vmem_limit_bytes=48 * 1024 * 1024),
        cost_estimate=pl.CostEstimate(
            flops=2 * 304 * blk * blk * half, bytes_accessed=20 << 20, transcendentals=0
        ),
        name="forward_tiles",
    )(rows, cols, srow, scol, sid, meta, scale, adj, *hist, *diff)


def backward_kernel(
    srow, scol, sid, scale, adj, z0, z1, z2, z3, z4, z5, z6, z7, z8,
    out, tiles, grads, acc, sems,
):
    copies = gather_copies((z0, z1, z2, z3, z4, z5, z6, z7, z8), grads, sems, 0)
    for copy in copies:
        copy.start()
    n = sid.shape[0]

    def fetch(s):
        return pltpu.make_async_copy(adj.at[sid[s]], tiles.at[s], sems.at[9 + s])

    def begin(s, carry):
        fetch(s).start()
        return carry

    lax.fori_loop(0, n, begin, 0)
    acc[...] = jnp.zeros_like(acc)
    for copy in copies:
        copy.wait()

    def finish(s, carry):
        fetch(s).wait()
        return carry

    lax.fori_loop(0, n, finish, 0)

    def body(g, carry):
        start = g * GROUP
        products = [
            lax.dot_general(
                tiles[start + u],
                grads[srow[start + u]],
                (((0,), (0,)), ((), ())),
                preferred_element_type=F32,
            )
            * scale[start + u]
            for u in range(GROUP)
        ]
        for u in range(GROUP):
            c = scol[start + u]
            acc[c] = acc[c] + products[u]
        return carry

    lax.fori_loop(0, n // GROUP, body, 0)
    out[...] = acc[...].astype(out.dtype)


def backward_tiles(srow, scol, sid, scale, adj, parts):
    _, blk, _ = adj.shape
    half = parts[0].shape[-1]
    n = sid.shape[0]
    return pl.pallas_call(
        backward_kernel,
        out_shape=jax.ShapeDtypeStruct((64, blk, half), BF),
        in_specs=[SMEM] * 4 + [HBM] * 10,
        out_specs=VMEM,
        scratch_shapes=[
            pltpu.VMEM((n, blk, blk), BF),
            pltpu.VMEM((32, blk, half), BF),
            pltpu.VMEM((64, blk, half), F32),
            pltpu.SemaphoreType.DMA((9 + n,)),
        ],
        compiler_params=pltpu.CompilerParams(vmem_limit_bytes=32 * 1024 * 1024),
        cost_estimate=pl.CostEstimate(
            flops=2 * n * blk * blk * half, bytes_accessed=8 << 20, transcendentals=0
        ),
        name="backward_tiles",
    )(srow, scol, sid, scale, adj, *parts)


def dense_kernel(z, zo, w, wo, d, do, out, dz, wg):
    half = d.shape[1]
    zv = z[...]
    pre = jnp.dot(zv, w[...], preferred_element_type=F32)
    pre += jnp.dot(zo[...], wo[...], preferred_element_type=F32)
    inner = 0.7978845608 * (pre + 0.044715 * pre * pre * pre)
    th = jnp.tanh(inner)
    cdf = 0.5 * (1.0 + th)
    out[...] = (pre * cdf)[:, :half].astype(out.dtype)
    slope = cdf + 0.5 * pre * (1.0 - th * th) * (
        0.7978845608 * (1.0 + 3.0 * 0.044715 * pre * pre)
    )
    cot = jnp.concatenate([d[...], do[...]], axis=1).astype(F32)
    g = (cot * slope).astype(BF)
    dz[...] = lax.dot_general(
        g, w[...], (((1,), (1,)), ((), ())), preferred_element_type=F32
    ).astype(BF)
    wg[...] = lax.dot_general(
        zv, g, (((0,), (0,)), ((), ())), preferred_element_type=F32
    ).astype(wg.dtype)


def dense(z, zo, w, wo, d, do):
    rows, half = z.shape
    return pl.pallas_call(
        dense_kernel,
        out_shape=[
            jax.ShapeDtypeStruct((rows, half), BF),
            jax.ShapeDtypeStruct((rows, half), BF),
            jax.ShapeDtypeStruct(w.shape, BF),
        ],
        in_specs=[VMEM] * 6,
        out_specs=[VMEM] * 3,
        compiler_params=pltpu.CompilerParams(vmem_limit_bytes=32 * 1024 * 1024),
        cost_estimate=pl.CostEstimate(
            flops=8 * rows * half * 2 * half, bytes_accessed=2 << 20, transcendentals=rows * half * 2
        ),
        name="dense",
    )(z, zo, w, wo, d, do)


def plus(a, b):
    return (a.astype(F32) + b.astype(F32)).astype(BF)


def gather_ring(x):
    blocks = {0: x}
    up = down = x
    for k in (1, 2, 3):
        up, down = shift(up, "z", 1), shift(down, "z", -1)
        blocks[8 - k], blocks[k] = up, down
    half = x.shape[0] // 2
    far_lo = shift(up[:half], "z", 1)
    far_hi = shift(down[half:], "z", -1)
    return [blocks[0], blocks[1], blocks[2], blocks[3], far_lo, far_hi, blocks[5], blocks[6], blocks[7]]


def local(
    fresh, history, adj_val, tile_row, tile_col, tile_count, samp_id, samp_scale, weight, d_out
):
    adj = adj_val[0, 0]
    rows = tile_row[0, 0]
    cols = tile_col[0, 0]
    count = tile_count[0, 0]
    sid = samp_id[0, 0]
    scale = samp_scale[0, 0]
    n_tiles, blk, _ = adj.shape
    half = fresh.shape[1]
    xpos, ypos, zpos = lax.axis_index("x"), lax.axis_index("y"), lax.axis_index("z")
    core = lax.axis_index("core")
    hist_in = history.reshape(4, blk, half)
    diff_in = (fresh.astype(F32) - history.astype(F32)).astype(BF).reshape(4, blk, half)
    hist = gather_two(hist_in, "x", "y")
    diff = gather_two(diff_in, "y", "x")

    xrel = (cols // 4 - xpos) % 4
    yrel = (cols // 16 - ypos) % 4
    hcol = (yrel * 4 + xrel) * 4 + cols % 4
    dcol = (xrel * 4 + yrel) * 4 + cols % 4
    live_row = jnp.where(jnp.arange(n_tiles, dtype=jnp.int32) < count, rows, 32)
    srow = rows[sid]
    meta = jnp.stack([count, zpos.astype(jnp.int32)])
    o4a, o4b, o3, o2, o1, o0, m1, m2, m3 = forward_tiles(
        live_row, hcol, srow, dcol[sid], sid, meta, scale, adj, hist, diff
    )

    up, down = shift(o4a, "z", 1), shift(o4b, "z", -1)
    up = shift(jnp.concatenate([plus(up, o3[:2]), o3[2:]], axis=0), "z", 1)
    down = shift(jnp.concatenate([m3[:2], plus(down, m3[2:])], axis=0), "z", -1)
    up, down = shift(plus(up, o2), "z", 1), shift(plus(down, m2), "z", -1)
    up, down = shift(plus(up, o1), "z", 1), shift(plus(down, m1), "z", -1)
    zval = (up.astype(F32) + down.astype(F32) + o0.astype(F32)).astype(BF)
    zval = zval.reshape(4 * blk, half)

    wrel = jnp.where(core == 0, weight, jnp.roll(weight, half, axis=1))
    wother = shift(weight, "core", 1)
    wother = jnp.where(core == 0, wother, jnp.roll(wother, half, axis=1))
    d_other = shift(d_out, "core", 1)
    zother = shift(zval, "core", 1)
    layer_out, dz, wpart = dense(zval, zother, wrel, wother, d_out, d_other)

    parts = gather_ring(dz.reshape(4, blk, half))
    row_rel = ((srow // 4 - zpos) % 8) * 4 + srow % 4
    back = backward_tiles(row_rel, cols[sid], sid, scale, adj, parts)
    back = lax.all_to_all(back, ("y", "x"), 0, 0, tiled=True)
    fresh_grad = back.reshape(16, 4 * blk, half).astype(F32).sum(0)

    wide = weight.shape[1]
    wparts = lax.all_to_all(wpart, "z", 0, 0, tiled=True)
    wsum = wparts.reshape(8, half // 8, wide).astype(F32).sum(0).astype(BF)
    wparts = lax.all_to_all(
        jnp.broadcast_to(wsum, (16,) + wsum.shape), ("y", "x"), 0, 0, tiled=True
    )
    wsum = wparts.astype(F32).sum(0).astype(BF)
    wgrad = lax.all_to_all(
        jnp.broadcast_to(wsum, (8,) + wsum.shape), "z", 0, 0, tiled=True
    )
    wgrad = wgrad.reshape(half, wide).astype(F32)
    wgrad = jnp.where(core == 0, wgrad, jnp.roll(wgrad, half, axis=1))
    return layer_out, wgrad, fresh_grad


def solution(mesh):
    fine = Mesh(mesh.devices.reshape(4, 4, 8, 2), ("y", "x", "z", "core"))
    row = ("y", "x")
    nodes = P(("y", "x", "z"), "core")
    placed = (
        nodes,
        nodes,
        P(row, "z", None, None, None),
        P(row, "z", None),
        P(row, "z", None),
        P(row, "z"),
        P(row, "z", None),
        P(row, "z", None),
        P("core", None),
        nodes,
    )
    return jax.shard_map(
        local,
        mesh=fine,
        in_specs=placed,
        out_specs=(nodes, P("core", None), nodes),
        check_vma=False,
    )
```

time: 704 us -> 250 us (0.36)
  waiting for transfers between devices: 462 us -> 109 us
  other arithmetic: 127 us -> 8.68 us
  starting transfers between devices: 0.29 us -> 86.4 us
  matrix products: 47.1 us -> 0 us
  local copies, waits for them, and re-layouts: 49.5 us -> 17.9 us
  Pallas kernels: 0 us -> 22 us
  between operations: 14.2 us -> 1.61 us
    psum x1 -> x0, waiting for transfers between devices: 220 us -> none  [local(): weight_grad = lax.psum(weight_part, ('row', 'col'))]
    reduce_scatter x3 -> x0, waiting for transfers between devices: 146 us -> none  [the longest x1 78.8 us: local(): lax.psum_scatter(back.astype(jnp.bfloat16), 'row', scatter_dimension=0, t...]
    scatter-add x10 -> x0, other arithmetic: 109 us -> none  [the longest x8 79.7 us: tile_step(): return total.at[part_rows].add(product * live[:, None, None])]
    all_gather x3 -> x0, waiting for transfers between devices: 94.3 us -> none  [the longest x1 51.8 us: local(): lax.all_gather(history, 'row', axis=0, tiled=True)]
    ppermute x0 -> x33, waiting for transfers between devices: none -> 56.1 us  [shift(): return lax.ppermute(x, axis, [(i, (i + step) % n) for i in range(n)])]
    ppermute x0 -> x33, starting transfers between devices: none -> 55.4 us  [shift(): return lax.ppermute(x, axis, [(i, (i + step) % n) for i in range(n)])]
    all_to_all x0 -> x4, waiting for transfers between devices: none -> 53 us  [the longest x1 43.7 us: local(): back = lax.all_to_all(back, ('y', 'x'), 0, 0, tiled=True)]
    dot_general x13 -> x0, matrix products: 47.1 us -> none  [the longest x8 31.3 us: tile_step(): jnp.einsum('tij,tjd->tid', part_vals, inputs, preferred_element_type=jnp....]
  transfers between devices with their start and end apart: 7 -> 37, of which waited for: 6 -> 19; matrix products, arithmetic and copies ran while one was open for 22% -> 7% of each run, Pallas kernels for 0% -> 3%
where the time goes in v1:
time: 250 us; the launch traced here: 246 us
  waiting for transfers between devices  109 us (44%)
  starting transfers between devices  86.4 us (35%)
  Pallas kernels  22 us (9%)
  local copies, waits for them, and re-layouts  17.9 us (7%)
  other arithmetic  8.68 us (3%)
    ppermute x33, waiting for transfers between devices, shift(): return lax.ppermute(x, axis, [(i, (i + step) % n) for i in range(n)])  56.1 us
    ppermute x33, starting transfers between devices, shift(): return lax.ppermute(x, axis, [(i, (i + step) % n) for i in range(n)])  55.4 us
    all_to_all x1, waiting for transfers between devices, local(): back = lax.all_to_all(back, ('y', 'x'), 0, 0, tiled=True)  43.7 us
    pallas_call x1, Pallas kernels, forward_tiles(): pl.pallas_call(forward_kernel, out_shape=[part, part, whole, whole, whole...  11.8 us
    all_to_all x1, starting transfers between devices, local(): lax.all_to_all(jnp.broadcast_to(wsum, (16,) + wsum.shape), ('y', 'x'), 0,...  11.6 us
    all_to_all x1, waiting for transfers between devices, local(): wparts = lax.all_to_all(wpart, 'z', 0, 0, tiled=True)  9.32 us
    all_to_all x1, starting transfers between devices, local(): wparts = lax.all_to_all(wpart, 'z', 0, 0, tiled=True)  8.8 us
    pallas_call x1, Pallas kernels, backward_tiles(): pl.pallas_call(backward_kernel, out_shape=jax.ShapeDtypeStruct((64, blk,...  7.29 us
  transfers between devices with their start and end apart: 37, of which 19 were waited for; matrix products, arithmetic and copies ran while one was open for 7% of the time, Pallas kernels for 3%

profile of v1, /device:TPU:2, one launch (start us, length us, event | category | flops | bytes accessed | tf_op | source)
XLA Modules:
  0.0 245.8 jit_solution(2285545790115066210)
XLA Ops:
  0.6 1.1 subtract_convert_fusion
  1.7 3.1 %collective-permute-start.7 = (bf16[4,128,256]{2,1,0:T(8,128)(2,1)S(1)}, bf16[4,128,256]{2,1,0:T(8,128)(2,1)S(1)}, u32[]{:S(2)}, u32[]{:S(2)}) collective-permute-start(bf16[4,128,256]{2,1,0:T(8,128)(2,1)S(1)} %bitcast.48), channel_id=1, source_target_pairs={{0,192},{64,0},{128,64},{192,128},{1,193},{65,1},{129,65},{193,129... | collective-permute-start | bytes 786440 | tf_op jit(solution)/shard_map/ppermute | solution.py:20
  4.8 0.6 collective-permute-start.8
  5.5 1.0 collective-permute-start.9
  6.4 0.5 collective-permute-start
  7.0 2.4 collective-permute-start.1
  9.4 6.6 %collective-permute-done.7 = bf16[4,128,256]{2,1,0:T(8,128)(2,1)S(1)} collective-permute-done((bf16[4,128,256]{2,1,0:T(8,128)(2,1)S(1)}, bf16[4,128,256]{2,1,0:T(8,128)(2,1)S(1)}, u32[]{:S(2)}, u32[]{:S(2)}) %collective-permute-start.7) | collective-permute-done | bytes 262176 | tf_op jit(solution)/shard_map/ppermute | solution.py:20
  16.0 1.5 collective-permute-start.2
  17.5 2.2 collective-permute-done.9
  19.9 1.6 collective-permute-start.11
  22.0 0.6 collective-permute-done.2
  22.6 1.1 pad_maximum_fusion.h0
  23.7 3.0 %collective-permute-start.4 = (bf16[16,128,256]{2,1,0:T(8,128)(2,1)S(1)}, bf16[16,128,256]{2,1,0:T(8,128)(2,1)}, u32[]{:S(2)}, u32[]{:S(2)}) collective-permute-start(bf16[16,128,256]{2,1,0:T(8,128)(2,1)S(1)} %pad_maximum_fusion.h0), channel_id=1, source_target_pairs={{0,64},{64,128},{128,192},{192,0},{1,65},{65,129},{129,193},{193,1... | collective-permute-start | bytes 3145736 | tf_op jit(solution)/shard_map/ppermute | solution.py:20
  26.7 3.7 %collective-permute-start.3 = (bf16[16,128,256]{2,1,0:T(8,128)(2,1)S(1)}, bf16[16,128,256]{2,1,0:T(8,128)(2,1)}, u32[]{:S(2)}, u32[]{:S(2)}) collective-permute-start(bf16[16,128,256]{2,1,0:T(8,128)(2,1)S(1)} %pad_maximum_fusion.h0), channel_id=1, source_target_pairs={{0,192},{64,0},{128,64},{192,128},{1,193},{65,1},{129,65},{193,129... | collective-permute-start | bytes 3145736 | tf_op jit(solution)/shard_map/ppermute | solution.py:20
  31.1 14.1 %collective-permute-done.11.d4 = bf16[16,128,256]{2,1,0:T(8,128)(2,1)} collective-permute-done((bf16[16,128,256]{2,1,0:T(8,128)(2,1)S(1)}, bf16[16,128,256]{2,1,0:T(8,128)(2,1)}, u32[]{:S(2)}, u32[]{:S(2)}) %collective-permute-start.11) | collective-permute-done | bytes 1048608 | tf_op jit(solution)/shard_map/ppermute | solution.py:20
  45.2 1.9 slice.76
  47.1 1.5 collective-permute-start.12
  48.6 1.9 slice.77
  50.4 1.6 collective-permute-start.13
  52.0 1.9 slice.74
  54.1 1.9 slice.75
  56.0 3.2 %collective-permute-start.6 = (bf16[8,128,256]{2,1,0:T(8,128)(2,1)}, bf16[8,128,256]{2,1,0:T(8,128)(2,1)S(1)}, u32[]{:S(2)}, u32[]{:S(2)}) collective-permute-start(bf16[8,128,256]{2,1,0:T(8,128)(2,1)} %slice.75), channel_id=1, source_target_pairs={{0,192},{64,0},{128,64},{192,128},{1,193},{65,1},{129,65},{193,129... | collective-permute-start | bytes 1572872 | tf_op jit(solution)/shard_map/ppermute | solution.py:20
  59.2 0.8 gather_fusion.1
  60.0 0.8 gather_fusion
  61.2 2.1 collective-permute-done.13.d3
  63.4 4.3 %collective-permute-done.5.h2 = bf16[8,128,256]{2,1,0:T(8,128)(2,1)S(1)} collective-permute-done((bf16[8,128,256]{2,1,0:T(8,128)(2,1)}, bf16[8,128,256]{2,1,0:T(8,128)(2,1)S(1)}, u32[]{:S(2)}, u32[]{:S(2)}) %collective-permute-start.5) | collective-permute-done | bytes 524320 | tf_op jit(solution)/shard_map/ppermute | solution.py:20
  67.7 1.8 collective-permute-done.6.h3
  69.5 11.8 %forward_tiles.1 = (bf16[2,128,256]{2,1,0:T(8,128)(2,1)S(1)}, bf16[2,128,256]{2,1,0:T(8,128)(2,1)S(1)}, bf16[4,128,256]{2,1,0:T(8,128)(2,1)S(1)}, bf16[4,128,256...) custom-call(s32[256]{0:T(256)S(1)} %get-tuple-element.36.rows, ...), custom_call_target="tpu_custom_call" | custom-call | flops 2550136832 | bytes 20971520 | tf_op jit(solution)/shard_map/forward_tiles/pallas_call | solution.py:123
  81.4 4.4 %collective-permute-start.18 = (bf16[2,128,256]{2,1,0:T(8,128)(2,1)S(1)}, bf16[2,128,256]{2,1,0:T(8,128)(2,1)S(1)}, u32[]{:S(2)}, u32[]{:S(2)}) collective-permute-start(bf16[2,128,256]{2,1,0:T(8,128)(2,1)S(1)} %get-tuple-element.20), channel_id=1, source_target_pairs={{0,14},{2,0},{4,2},{6,4},{8,6},{10,8},{12,10},{14,12},{1,15},{3,1}... | collective-permute-start | bytes 393224 | tf_op jit(solution)/shard_map/ppermute | solution.py:20
  85.8 2.8 %collective-permute-done.14 = bf16[2,128,256]{2,1,0:T(8,128)(2,1)S(1)} collective-permute-done((bf16[2,128,256]{2,1,0:T(8,128)(2,1)S(1)}, bf16[2,128,256]{2,1,0:T(8,128)(2,1)S(1)}, u32[]{:S(2)}, u32[]{:S(2)}) %collective-permute-start.14) | collective-permute-done | bytes 131104 | tf_op jit(solution)/shard_map/ppermute | solution.py:20
  88.9 3.8 %collective-permute-start.19 = (bf16[4,128,256]{2,1,0:T(8,128)(2,1)S(1)}, bf16[4,128,256]{2,1,0:T(8,128)(2,1)S(1)}, u32[]{:S(2)}, u32[]{:S(2)}) collective-permute-start(bf16[4,128,256]{2,1,0:T(8,128)(2,1)S(1)} %pad_maximum_fusion.3), channel_id=1, source_target_pairs={{0,14},{2,0},{4,2},{6,4},{8,6},{10,8},{12,10},{14,12},{1,15},{3,1}... | collective-permute-start | bytes 786440 | tf_op jit(solution)/shard_map/ppermute | solution.py:20
  92.7 4.2 %collective-permute-done.15 = bf16[4,128,256]{2,1,0:T(8,128)(2,1)S(1)} collective-permute-done((bf16[4,128,256]{2,1,0:T(8,128)(2,1)S(1)}, bf16[4,128,256]{2,1,0:T(8,128)(2,1)S(1)}, u32[]{:S(2)}, u32[]{:S(2)}) %collective-permute-start.15) | collective-permute-done | bytes 262176 | tf_op jit(solution)/shard_map/ppermute | solution.py:20
  97.5 2.9 %collective-permute-start.20 = (bf16[4,128,256]{2,1,0:T(8,128)(2,1)S(1)}, bf16[4,128,256]{2,1,0:T(8,128)(2,1)S(1)}, u32[]{:S(2)}, u32[]{:S(2)}) collective-permute-start(bf16[4,128,256]{2,1,0:T(8,128)(2,1)S(1)} %add_convert_fusion.2), channel_id=1, source_target_pairs={{0,14},{2,0},{4,2},{6,4},{8,6},{10,8},{12,10},{14,12},{1,15},{3,1}... | collective-permute-start | bytes 786440 | tf_op jit(solution)/shard_map/ppermute | solution.py:20
  100.9 3.7 %collective-permute-done.16 = bf16[4,128,256]{2,1,0:T(8,128)(2,1)S(1)} collective-permute-done((bf16[4,128,256]{2,1,0:T(8,128)(2,1)S(1)}, bf16[4,128,256]{2,1,0:T(8,128)(2,1)S(1)}, u32[]{:S(2)}, u32[]{:S(2)}) %collective-permute-start.16) | collective-permute-done | bytes 262176 | tf_op jit(solution)/shard_map/ppermute | solution.py:20
  104.8 3.3 %collective-permute-start.21 = (bf16[4,128,256]{2,1,0:T(8,128)(2,1)S(1)}, bf16[4,128,256]{2,1,0:T(8,128)(2,1)S(1)}, u32[]{:S(2)}, u32[]{:S(2)}) collective-permute-start(bf16[4,128,256]{2,1,0:T(8,128)(2,1)S(1)} %add_convert_fusion.1), channel_id=1, source_target_pairs={{0,14},{2,0},{4,2},{6,4},{8,6},{10,8},{12,10},{14,12},{1,15},{3,1}... | collective-permute-start | bytes 786440 | tf_op jit(solution)/shard_map/ppermute | solution.py:20
  108.1 1.0 fusion.8
  109.1 1.0 maximum_select_fusion.1.w
  110.2 2.2 collective-permute-done.17
  112.6 1.4 collective-permute-done.22.zo
  114.0 2.9 %dense.1 = (bf16[512,256]{1,0:T(8,128)(2,1)}, bf16[512,256]{1,0:T(8,128)(2,1)S(1)}, bf16[256,512]{1,0:T(8,128)(2,1)}) custom-call(bf16[512,256]{1,0:T(8,128)(2,1)S(1)} %bitcast.34, bf16[512,256]{1,0:T(8,128)(2,1)S(1)} %collective-permute-done.22.zo, bf16[256,512]{1,0:T(8,128)(2,1)S(1)} %maximum_select_fusion.1.w, ...), custom_call_target="tpu_custom_call" | custom-call | flops 536870912 | bytes 2097152 | tf_op jit(solution)/shard_map/dense/pallas_call | solution.py:238
  116.9 8.8 %all-to-all-start = ((bf16[8,32,512]{2,1,0:T(8,128)(2,1)}), bf16[8,32,512]{2,1,0:T(8,128)(2,1)S(1)}, u32[]{:S(2)}, u32[]{:S(2)}) async-start(bf16[8,32,512]{2,1,0:T(8,128)(2,1)} %bitcast.13), calls=%async_computation | async-start | bytes 524288 | tf_op jit(solution)/shard_map/all_to_all | solution.py:322
  125.7 2.0 collective-permute-start.28
  127.8 1.2 collective-permute-start.25
  129.0 9.3 %all-to-all-done = bf16[8,32,512]{2,1,0:T(8,128)(2,1)S(1)} async-done(((bf16[8,32,512]{2,1,0:T(8,128)(2,1)}), bf16[8,32,512]{2,1,0:T(8,128)(2,1)S(1)}, u32[]{:S(2)}, u32[]{:S(2)}) %all-to-all-start) | async-done | bytes 262176 | tf_op jit(solution)/shard_map/all_to_all | solution.py:322
  138.4 0.8 broadcast_in_dim.14
  139.2 11.6 %all-to-all-start.1 = ((bf16[16,32,512]{2,1,0:T(8,128)(2,1)}), bf16[16,32,512]{2,1,0:T(8,128)(2,1)S(1)}, u32[]{:S(2)}, u32[]{:S(2)}) async-start(bf16[16,32,512]{2,1,0:T(8,128)(2,1)} %broadcast_in_dim.14), calls=%async_computation.1 | async-start | bytes 1048576 | tf_op jit(solution)/shard_map/all_to_all | solution.py:324
  150.8 1.0 collective-permute-start.29
  151.8 2.3 collective-permute-start.26
  154.1 4.3 %collective-permute-done.29.z7 = bf16[4,128,256]{2,1,0:T(8,128)(2,1)S(1)} collective-permute-done((bf16[4,128,256]{2,1,0:T(8,128)(2,1)S(1)}, bf16[4,128,256]{2,1,0:T(8,128)(2,1)S(1)}, u32[]{:S(2)}, u32[]{:S(2)}) %collective-permute-start.29) | collective-permute-done | bytes 262176 | tf_op jit(solution)/shard_map/ppermute | solution.py:20
  158.4 3.2 %collective-permute-start.27 = (bf16[4,128,256]{2,1,0:T(8,128)(2,1)S(1)}, bf16[4,128,256]{2,1,0:T(8,128)(2,1)S(1)}, u32[]{:S(2)}, u32[]{:S(2)}) collective-permute-start(bf16[4,128,256]{2,1,0:T(8,128)(2,1)S(1)} %collective-permute-done.26.z2), channel_id=1, source_target_pairs={{0,14},{2,0},{4,2},{6,4},{8,6},{10,8},{12,10},{14,12},{1,15},{3,1}... | collective-permute-start | bytes 786440 | tf_op jit(solution)/shard_map/ppermute | solution.py:20
  161.8 0.7 broadcast_in_dim.15
  162.5 3.4 %all-to-all-start.2 = ((bf16[8,32,512]{2,1,0:T(8,128)(2,1)}), bf16[8,32,512]{2,1,0:T(8,128)(2,1)S(1)}, u32[]{:S(2)}, u32[]{:S(2)}) async-start(bf16[8,32,512]{2,1,0:T(8,128)(2,1)} %broadcast_in_dim.15), calls=%async_computation.2 | async-start | bytes 524288 | tf_op jit(solution)/shard_map/all_to_all | solution.py:328
  165.9 0.8 gather_fusion.2
  166.7 2.0 collective-permute-start.31
  168.7 2.5 %collective-permute-done.27.z3 = bf16[4,128,256]{2,1,0:T(8,128)(2,1)S(1)} collective-permute-done((bf16[4,128,256]{2,1,0:T(8,128)(2,1)S(1)}, bf16[4,128,256]{2,1,0:T(8,128)(2,1)S(1)}, u32[]{:S(2)}, u32[]{:S(2)}) %collective-permute-start.27) | collective-permute-done | bytes 262176 | tf_op jit(solution)/shard_map/ppermute | solution.py:20
  171.2 3.7 %collective-permute-start.32 = (bf16[2,128,256]{2,1,0:T(8,128)(2,1)S(1)}, bf16[2,128,256]{2,1,0:T(8,128)(2,1)S(1)}, u32[]{:S(2)}, u32[]{:S(2)}) collective-permute-start(bf16[2,128,256]{2,1,0:T(8,128)(2,1)S(1)} %slice.83), channel_id=1, source_target_pairs={{0,14},{2,0},{4,2},{6,4},{8,6},{10,8},{12,10},{14,12},{1,15},{3,1}... | collective-permute-start | bytes 393224 | tf_op jit(solution)/shard_map/ppermute | solution.py:20
  175.0 2.5 collective-permute-done.32.z5
  177.5 3.4 %copy-done = bf16[1,1,256,128,128]{4,3,2,1,0:T(8,128)(2,1)S(1)} copy-done((bf16[1,1,256,128,128]{4,3,2,1,0:T(8,128)(2,1)S(1)}, bf16[1,1,256,128,128]{4,3,2,1,0:T(8,128)(2,1)}, u32[]{:S(2)}) %copy-start) | copy-done | bytes 8388632
  180.9 7.3 %backward_tiles.1 = bf16[64,128,256]{2,1,0:T(8,128)(2,1)S(1)} custom-call(s32[48]{0:T(128)S(1)} %fusion.2.srow, s32[48]{0:T(128)S(1)} %gather_fusion.2, s32[48]{0:T(128)S(1)} %bitcast.36, f32[48]{0:T(128)S(1)} %bitcast.38, bf16[256,128,128]{2,1,0:T(8,128)(2,1)S(1)} %bitcast.29, bf16[4,128,256]{2,1,0:T(8,128)(2,1)S(1)} %bitcast.32, ...), custom_call_target="tpu_custom_call" | custom-call | flops 402653184 | bytes 8388608 | tf_op jit(solution)/shard_map/backward_tiles/pallas_call | solution.py:195
  188.2 2.0 copy-done.1
  190.2 7.2 %all-to-all-start.3 = ((bf16[64,128,256]{2,1,0:T(8,128)(2,1)}), bf16[64,128,256]{2,1,0:T(8,128)(2,1)}, u32[]{:S(2)}, u32[]{:S(2)}) async-start(bf16[64,128,256]{2,1,0:T(8,128)(2,1)} %copy-done.1), calls=%async_computation.3 | async-start | bytes 8388608 | tf_op jit(solution)/shard_map/all_to_all | solution.py:318
  197.5 0.9 maximum_select_fusion
  198.4 43.7 %all-to-all-done.3 = bf16[64,128,256]{2,1,0:T(8,128)(2,1)} async-done(((bf16[64,128,256]{2,1,0:T(8,128)(2,1)}), bf16[64,128,256]{2,1,0:T(8,128)(2,1)}, u32[]{:S(2)}, u32[]{:S(2)}) %all-to-all-start.3) | async-done | bytes 4194336 | tf_op jit(solution)/shard_map/all_to_all | solution.py:318
  242.1 3.6 %convert_reduce_fusion = f32[512,256]{1,0:T(8,128)} fusion(bf16[16,512,256]{2,1,0:T(8,128)(2,1)} %bitcast.25), kind=kLoop, calls=%fused_computation.3 | loop fusion | flops 4063232 | bytes 4718592 | tf_op jit(solution)/shard_map/reduce_sum | solution.py:319
  (68 shorter events, 3.6 us)
Async XLA Ops:
  0.6 30.4 %copy-start.2 = (s32[1,1,48]{2,1,0:T(1,128)S(1)}, s32[1,1,48]{2,1,0:T(1,128)}, u32[]{:S(2)}) copy-start(s32[1,1,48]{2,1,0:T(1,128)} %param.16) | copy-start | bytes 580
  1.7 14.3 %collective-permute-start.7 = (bf16[4,128,256]{2,1,0:T(8,128)(2,1)S(1)}, bf16[4,128,256]{2,1,0:T(8,128)(2,1)S(1)}, u32[]{:S(2)}, u32[]{:S(2)}) collective-permute-start(bf16[4,128,256]{2,1,0:T(8,128)(2,1)S(1)} %bitcast.48), channel_id=1, source_target_pairs={{0,192},{64,0},{128,64},{192,128},{1,193},{65,1},{129,65},{193,129... | collective-permute-start | bytes 786440 | tf_op jit(solution)/shard_map/ppermute | solution.py:20
  4.8 12.7 %collective-permute-start.8 = (bf16[4,128,256]{2,1,0:T(8,128)(2,1)S(1)}, bf16[4,128,256]{2,1,0:T(8,128)(2,1)S(1)}, u32[]{:S(2)}, u32[]{:S(2)}) collective-permute-start(bf16[4,128,256]{2,1,0:T(8,128)(2,1)S(1)} %bitcast.49), channel_id=1, source_target_pairs={{0,128},{64,192},{128,0},{192,64},{1,129},{65,193},{129,1},{193,65... | collective-permute-start | bytes 786440 | tf_op jit(solution)/shard_map/ppermute | solution.py:20
  5.5 14.3 %collective-permute-start.9 = (bf16[4,128,256]{2,1,0:T(8,128)(2,1)S(1)}, bf16[4,128,256]{2,1,0:T(8,128)(2,1)S(1)}, u32[]{:S(2)}, u32[]{:S(2)}) collective-permute-start(bf16[4,128,256]{2,1,0:T(8,128)(2,1)S(1)} %bitcast.50), channel_id=1, source_target_pairs={{0,64},{64,128},{128,192},{192,0},{1,65},{65,129},{129,193},{193,1... | collective-permute-start | bytes 786440 | tf_op jit(solution)/shard_map/ppermute | solution.py:20
  6.4 52.8 %copy-start.4 = (s32[1,1,256]{2,1,0:T(1,128)S(1)}, s32[1,1,256]{2,1,0:T(1,128)}, u32[]{:S(2)}) copy-start(s32[1,1,256]{2,1,0:T(1,128)} %param.14) | copy-start | bytes 3076
  6.4 53.6 %copy-start.5 = (s32[1,1,256]{2,1,0:T(1,128)S(1)}, s32[1,1,256]{2,1,0:T(1,128)}, u32[]{:S(2)}) copy-start(s32[1,1,256]{2,1,0:T(1,128)} %param.13) | copy-start | bytes 3076
  6.4 15.5 %collective-permute-start = (bf16[4,128,256]{2,1,0:T(8,128)(2,1)}, bf16[4,128,256]{2,1,0:T(8,128)(2,1)S(1)}, u32[]{:S(2)}, u32[]{:S(2)}) collective-permute-start(bf16[4,128,256]{2,1,0:T(8,128)(2,1)} %bitcast.44), channel_id=1, source_target_pairs={{0,48},{16,0},{32,16},{48,32},{1,49},{17,1},{33,17},{49,33},{2,50}... | collective-permute-start | bytes 786440 | tf_op jit(solution)/shard_map/ppermute | solution.py:20
  7.0 15.0 %collective-permute-start.1 = (bf16[4,128,256]{2,1,0:T(8,128)(2,1)}, bf16[4,128,256]{2,1,0:T(8,128)(2,1)S(1)}, u32[]{:S(2)}, u32[]{:S(2)}) collective-permute-start(bf16[4,128,256]{2,1,0:T(8,128)(2,1)} %bitcast.45), channel_id=1, source_target_pairs={{0,32},{16,48},{32,0},{48,16},{1,33},{17,49},{33,1},{49,17},{2,34}... | collective-permute-start | bytes 786440 | tf_op jit(solution)/shard_map/ppermute | solution.py:20
  16.0 6.6 %collective-permute-start.2 = (bf16[4,128,256]{2,1,0:T(8,128)(2,1)}, bf16[4,128,256]{2,1,0:T(8,128)(2,1)S(1)}, u32[]{:S(2)}, u32[]{:S(2)}) collective-permute-start(bf16[4,128,256]{2,1,0:T(8,128)(2,1)} %bitcast.46), channel_id=1, source_target_pairs={{0,16},{16,32},{32,48},{48,0},{1,17},{17,33},{33,49},{49,1},{2,18}... | collective-permute-start | bytes 786440 | tf_op jit(solution)/shard_map/ppermute | solution.py:20
  19.9 28.7 %copy-start.6 = (bf16[16,128,256]{2,1,0:T(8,128)(2,1)}, bf16[16,128,256]{2,1,0:T(8,128)(2,1)S(1)}, u32[]{:S(2)}) copy-start(bf16[16,128,256]{2,1,0:T(8,128)(2,1)S(1)} %pad_maximum_fusion.1.d0) | copy-start | bytes 3145732
  19.9 49.6 %copy-start.3 = (f32[1,1,48]{2,1,0:T(1,128)S(1)}, f32[1,1,48]{2,1,0:T(1,128)}, u32[]{:S(2)}) copy-start(f32[1,1,48]{2,1,0:T(1,128)} %param.17) | copy-start | bytes 580
  19.9 25.3 %collective-permute-start.11 = (bf16[16,128,256]{2,1,0:T(8,128)(2,1)S(1)}, bf16[16,128,256]{2,1,0:T(8,128)(2,1)}, u32[]{:S(2)}, u32[]{:S(2)}) collective-permute-start(bf16[16,128,256]{2,1,0:T(8,128)(2,1)S(1)} %pad_maximum_fusion.1.d0), channel_id=1, source_target_pairs={{0,16},{16,32},{32,48},{48,0},{1,17},{17,33},{33,49},{49,1},{2,18}... | collective-permute-start | bytes 3145736 | tf_op jit(solution)/shard_map/ppermute | solution.py:20
  21.4 27.1 %collective-permute-start.10 = (bf16[16,128,256]{2,1,0:T(8,128)(2,1)S(1)}, bf16[16,128,256]{2,1,0:T(8,128)(2,1)}, u32[]{:S(2)}, u32[]{:S(2)}) collective-permute-start(bf16[16,128,256]{2,1,0:T(8,128)(2,1)S(1)} %pad_maximum_fusion.1.d0), channel_id=1, source_target_pairs={{0,48},{16,0},{32,16},{48,32},{1,49},{17,1},{33,17},{49,33},{2,50}... | collective-permute-start | bytes 3145736 | tf_op jit(solution)/shard_map/ppermute | solution.py:20
  23.7 28.3 %collective-permute-start.4 = (bf16[16,128,256]{2,1,0:T(8,128)(2,1)S(1)}, bf16[16,128,256]{2,1,0:T(8,128)(2,1)}, u32[]{:S(2)}, u32[]{:S(2)}) collective-permute-start(bf16[16,128,256]{2,1,0:T(8,128)(2,1)S(1)} %pad_maximum_fusion.h0), channel_id=1, source_target_pairs={{0,64},{64,128},{128,192},{192,0},{1,65},{65,129},{129,193},{193,1... | collective-permute-start | bytes 3145736 | tf_op jit(solution)/shard_map/ppermute | solution.py:20
  26.7 27.4 %collective-permute-start.3 = (bf16[16,128,256]{2,1,0:T(8,128)(2,1)S(1)}, bf16[16,128,256]{2,1,0:T(8,128)(2,1)}, u32[]{:S(2)}, u32[]{:S(2)}) collective-permute-start(bf16[16,128,256]{2,1,0:T(8,128)(2,1)S(1)} %pad_maximum_fusion.h0), channel_id=1, source_target_pairs={{0,192},{64,0},{128,64},{192,128},{1,193},{65,1},{129,65},{193,129... | collective-permute-start | bytes 3145736 | tf_op jit(solution)/shard_map/ppermute | solution.py:20
  47.1 14.2 %collective-permute-start.12 = (bf16[8,128,256]{2,1,0:T(8,128)(2,1)}, bf16[8,128,256]{2,1,0:T(8,128)(2,1)S(1)}, u32[]{:S(2)}, u32[]{:S(2)}) collective-permute-start(bf16[8,128,256]{2,1,0:T(8,128)(2,1)} %slice.76), channel_id=1, source_target_pairs={{0,16},{16,32},{32,48},{48,0},{1,17},{17,33},{33,49},{49,1},{2,18}... | collective-permute-start | bytes 1572872 | tf_op jit(solution)/shard_map/ppermute | solution.py:20
  50.4 13.0 %collective-permute-start.13 = (bf16[8,128,256]{2,1,0:T(8,128)(2,1)}, bf16[8,128,256]{2,1,0:T(8,128)(2,1)S(1)}, u32[]{:S(2)}, u32[]{:S(2)}) collective-permute-start(bf16[8,128,256]{2,1,0:T(8,128)(2,1)} %slice.77), channel_id=1, source_target_pairs={{0,48},{16,0},{32,16},{48,32},{1,49},{17,1},{33,17},{49,33},{2,50}... | collective-permute-start | bytes 1572872 | tf_op jit(solution)/shard_map/ppermute | solution.py:20
  53.9 13.8 %collective-permute-start.5 = (bf16[8,128,256]{2,1,0:T(8,128)(2,1)}, bf16[8,128,256]{2,1,0:T(8,128)(2,1)S(1)}, u32[]{:S(2)}, u32[]{:S(2)}) collective-permute-start(bf16[8,128,256]{2,1,0:T(8,128)(2,1)} %slice.74), channel_id=1, source_target_pairs={{0,64},{64,128},{128,192},{192,0},{1,65},{65,129},{129,193},{193,1... | collective-permute-start | bytes 1572872 | tf_op jit(solution)/shard_map/ppermute | solution.py:20
  56.0 13.5 %collective-permute-start.6 = (bf16[8,128,256]{2,1,0:T(8,128)(2,1)}, bf16[8,128,256]{2,1,0:T(8,128)(2,1)S(1)}, u32[]{:S(2)}, u32[]{:S(2)}) collective-permute-start(bf16[8,128,256]{2,1,0:T(8,128)(2,1)} %slice.75), channel_id=1, source_target_pairs={{0,192},{64,0},{128,64},{192,128},{1,193},{65,1},{129,65},{193,129... | collective-permute-start | bytes 1572872 | tf_op jit(solution)/shard_map/ppermute | solution.py:20
  81.3 7.4 %collective-permute-start.14 = (bf16[2,128,256]{2,1,0:T(8,128)(2,1)S(1)}, bf16[2,128,256]{2,1,0:T(8,128)(2,1)S(1)}, u32[]{:S(2)}, u32[]{:S(2)}) collective-permute-start(bf16[2,128,256]{2,1,0:T(8,128)(2,1)S(1)} %get-tuple-element.15), channel_id=1, source_target_pairs={{0,2},{2,4},{4,6},{6,8},{8,10},{10,12},{12,14},{14,0},{1,3},{3,5},... | collective-permute-start | bytes 393224 | tf_op jit(solution)/shard_map/ppermute | solution.py:20
  81.4 7.4 %collective-permute-start.18 = (bf16[2,128,256]{2,1,0:T(8,128)(2,1)S(1)}, bf16[2,128,256]{2,1,0:T(8,128)(2,1)S(1)}, u32[]{:S(2)}, u32[]{:S(2)}) collective-permute-start(bf16[2,128,256]{2,1,0:T(8,128)(2,1)S(1)} %get-tuple-element.20), channel_id=1, source_target_pairs={{0,14},{2,0},{4,2},{6,4},{8,6},{10,8},{12,10},{14,12},{1,15},{3,1}... | collective-permute-start | bytes 393224 | tf_op jit(solution)/shard_map/ppermute | solution.py:20
  88.7 8.1 %collective-permute-start.15 = (bf16[4,128,256]{2,1,0:T(8,128)(2,1)S(1)}, bf16[4,128,256]{2,1,0:T(8,128)(2,1)S(1)}, u32[]{:S(2)}, u32[]{:S(2)}) collective-permute-start(bf16[4,128,256]{2,1,0:T(8,128)(2,1)S(1)} %pad_maximum_fusion.2), channel_id=1, source_target_pairs={{0,2},{2,4},{4,6},{6,8},{8,10},{10,12},{12,14},{14,0},{1,3},{3,5},... | collective-permute-start | bytes 786440 | tf_op jit(solution)/shard_map/ppermute | solution.py:20
  88.9 8.5 %collective-permute-start.19 = (bf16[4,128,256]{2,1,0:T(8,128)(2,1)S(1)}, bf16[4,128,256]{2,1,0:T(8,128)(2,1)S(1)}, u32[]{:S(2)}, u32[]{:S(2)}) collective-permute-start(bf16[4,128,256]{2,1,0:T(8,128)(2,1)S(1)} %pad_maximum_fusion.3), channel_id=1, source_target_pairs={{0,14},{2,0},{4,2},{6,4},{8,6},{10,8},{12,10},{14,12},{1,15},{3,1}... | collective-permute-start | bytes 786440 | tf_op jit(solution)/shard_map/ppermute | solution.py:20
  96.9 7.7 %collective-permute-start.16 = (bf16[4,128,256]{2,1,0:T(8,128)(2,1)S(1)}, bf16[4,128,256]{2,1,0:T(8,128)(2,1)S(1)}, u32[]{:S(2)}, u32[]{:S(2)}) collective-permute-start(bf16[4,128,256]{2,1,0:T(8,128)(2,1)S(1)} %add_convert_fusion.4), channel_id=1, source_target_pairs={{0,2},{2,4},{4,6},{6,8},{8,10},{10,12},{12,14},{14,0},{1,3},{3,5},... | collective-permute-start | bytes 786440 | tf_op jit(solution)/shard_map/ppermute | solution.py:20
  97.5 7.3 %collective-permute-start.20 = (bf16[4,128,256]{2,1,0:T(8,128)(2,1)S(1)}, bf16[4,128,256]{2,1,0:T(8,128)(2,1)S(1)}, u32[]{:S(2)}, u32[]{:S(2)}) collective-permute-start(bf16[4,128,256]{2,1,0:T(8,128)(2,1)S(1)} %add_convert_fusion.2), channel_id=1, source_target_pairs={{0,14},{2,0},{4,2},{6,4},{8,6},{10,8},{12,10},{14,12},{1,15},{3,1}... | collective-permute-start | bytes 786440 | tf_op jit(solution)/shard_map/ppermute | solution.py:20
  100.4 12.1 %collective-permute-start.23 = (bf16[256,512]{1,0:T(8,128)(2,1)}, bf16[256,512]{1,0:T(8,128)(2,1)S(1)}, u32[]{:S(2)}, u32[]{:S(2)}) collective-permute-start(bf16[256,512]{1,0:T(8,128)(2,1)} %param.18), channel_id=1, source_target_pairs={{0,1},{1,0},{2,3},{3,2},{4,5},{5,4},{6,7},{7,6},{8,9},{9,8},{10,11... | collective-permute-start | bytes 786440 | tf_op jit(solution)/shard_map/ppermute | solution.py:20
  100.4 12.2 %collective-permute-start.24 = (bf16[512,256]{1,0:T(8,128)(2,1)}, bf16[512,256]{1,0:T(8,128)(2,1)S(1)}, u32[]{:S(2)}, u32[]{:S(2)}) collective-permute-start(bf16[512,256]{1,0:T(8,128)(2,1)} %d.1), channel_id=1, source_target_pairs={{0,1},{1,0},{2,3},{3,2},{4,5},{5,4},{6,7},{7,6},{8,9},{9,8},{10,11... | collective-permute-start | bytes 786440 | tf_op jit(solution)/shard_map/ppermute | solution.py:20
  104.7 7.7 %collective-permute-start.17 = (bf16[4,128,256]{2,1,0:T(8,128)(2,1)S(1)}, bf16[4,128,256]{2,1,0:T(8,128)(2,1)S(1)}, u32[]{:S(2)}, u32[]{:S(2)}) collective-permute-start(bf16[4,128,256]{2,1,0:T(8,128)(2,1)S(1)} %add_convert_fusion.3), channel_id=1, source_target_pairs={{0,2},{2,4},{4,6},{6,8},{8,10},{10,12},{12,14},{14,0},{1,3},{3,5},... | collective-permute-start | bytes 786440 | tf_op jit(solution)/shard_map/ppermute | solution.py:20
  104.8 7.5 %collective-permute-start.21 = (bf16[4,128,256]{2,1,0:T(8,128)(2,1)S(1)}, bf16[4,128,256]{2,1,0:T(8,128)(2,1)S(1)}, u32[]{:S(2)}, u32[]{:S(2)}) collective-permute-start(bf16[4,128,256]{2,1,0:T(8,128)(2,1)S(1)} %add_convert_fusion.1), channel_id=1, source_target_pairs={{0,14},{2,0},{4,2},{6,4},{8,6},{10,8},{12,10},{14,12},{1,15},{3,1}... | collective-permute-start | bytes 786440 | tf_op jit(solution)/shard_map/ppermute | solution.py:20
  112.4 1.6 collective-permute-start.22
  116.9 21.4 %all-to-all-start = ((bf16[8,32,512]{2,1,0:T(8,128)(2,1)}), bf16[8,32,512]{2,1,0:T(8,128)(2,1)S(1)}, u32[]{:S(2)}, u32[]{:S(2)}) async-start(bf16[8,32,512]{2,1,0:T(8,128)(2,1)} %bitcast.13), calls=%async_computation | async-start | bytes 524288 | tf_op jit(solution)/shard_map/all_to_all | solution.py:322
  125.7 25.0 %collective-permute-start.28 = (bf16[4,128,256]{2,1,0:T(8,128)(2,1)S(1)}, bf16[4,128,256]{2,1,0:T(8,128)(2,1)S(1)}, u32[]{:S(2)}, u32[]{:S(2)}) collective-permute-start(bf16[4,128,256]{2,1,0:T(8,128)(2,1)S(1)} %bitcast.30), channel_id=1, source_target_pairs={{0,2},{2,4},{4,6},{6,8},{8,10},{10,12},{12,14},{14,0},{1,3},{3,5},... | collective-permute-start | bytes 786440 | tf_op jit(solution)/shard_map/ppermute | solution.py:20
  127.8 24.0 %collective-permute-start.25 = (bf16[4,128,256]{2,1,0:T(8,128)(2,1)S(1)}, bf16[4,128,256]{2,1,0:T(8,128)(2,1)S(1)}, u32[]{:S(2)}, u32[]{:S(2)}) collective-permute-start(bf16[4,128,256]{2,1,0:T(8,128)(2,1)S(1)} %bitcast.31), channel_id=1, source_target_pairs={{0,14},{2,0},{4,2},{6,4},{8,6},{10,8},{12,10},{14,12},{1,15},{3,1}... | collective-permute-start | bytes 786440 | tf_op jit(solution)/shard_map/ppermute | solution.py:20
  139.2 22.5 %all-to-all-start.1 = ((bf16[16,32,512]{2,1,0:T(8,128)(2,1)}), bf16[16,32,512]{2,1,0:T(8,128)(2,1)S(1)}, u32[]{:S(2)}, u32[]{:S(2)}) async-start(bf16[16,32,512]{2,1,0:T(8,128)(2,1)} %broadcast_in_dim.14), calls=%async_computation.1 | async-start | bytes 1048576 | tf_op jit(solution)/shard_map/all_to_all | solution.py:324
  150.8 7.7 %collective-permute-start.29 = (bf16[4,128,256]{2,1,0:T(8,128)(2,1)S(1)}, bf16[4,128,256]{2,1,0:T(8,128)(2,1)S(1)}, u32[]{:S(2)}, u32[]{:S(2)}) collective-permute-start(bf16[4,128,256]{2,1,0:T(8,128)(2,1)S(1)} %collective-permute-done.28.z8), channel_id=1, source_target_pairs={{0,2},{2,4},{4,6},{6,8},{8,10},{10,12},{12,14},{14,0},{1,3},{3,5},... | collective-permute-start | bytes 786440 | tf_op jit(solution)/shard_map/ppermute | solution.py:20
  151.8 6.7 %collective-permute-start.26 = (bf16[4,128,256]{2,1,0:T(8,128)(2,1)S(1)}, bf16[4,128,256]{2,1,0:T(8,128)(2,1)S(1)}, u32[]{:S(2)}, u32[]{:S(2)}) collective-permute-start(bf16[4,128,256]{2,1,0:T(8,128)(2,1)S(1)} %collective-permute-done.25.z1), channel_id=1, source_target_pairs={{0,14},{2,0},{4,2},{6,4},{8,6},{10,8},{12,10},{14,12},{1,15},{3,1}... | collective-permute-start | bytes 786440 | tf_op jit(solution)/shard_map/ppermute | solution.py:20
  158.4 8.3 %collective-permute-start.30 = (bf16[4,128,256]{2,1,0:T(8,128)(2,1)S(1)}, bf16[4,128,256]{2,1,0:T(8,128)(2,1)S(1)}, u32[]{:S(2)}, u32[]{:S(2)}) collective-permute-start(bf16[4,128,256]{2,1,0:T(8,128)(2,1)S(1)} %collective-permute-done.29.z7), channel_id=1, source_target_pairs={{0,2},{2,4},{4,6},{6,8},{8,10},{10,12},{12,14},{14,0},{1,3},{3,5},... | collective-permute-start | bytes 786440 | tf_op jit(solution)/shard_map/ppermute | solution.py:20
  158.4 12.8 %collective-permute-start.27 = (bf16[4,128,256]{2,1,0:T(8,128)(2,1)S(1)}, bf16[4,128,256]{2,1,0:T(8,128)(2,1)S(1)}, u32[]{:S(2)}, u32[]{:S(2)}) collective-permute-start(bf16[4,128,256]{2,1,0:T(8,128)(2,1)S(1)} %collective-permute-done.26.z2), channel_id=1, source_target_pairs={{0,14},{2,0},{4,2},{6,4},{8,6},{10,8},{12,10},{14,12},{1,15},{3,1}... | collective-permute-start | bytes 786440 | tf_op jit(solution)/shard_map/ppermute | solution.py:20
  162.5 27.7 %all-to-all-start.2 = ((bf16[8,32,512]{2,1,0:T(8,128)(2,1)}), bf16[8,32,512]{2,1,0:T(8,128)(2,1)S(1)}, u32[]{:S(2)}, u32[]{:S(2)}) async-start(bf16[8,32,512]{2,1,0:T(8,128)(2,1)} %broadcast_in_dim.15), calls=%async_computation.2 | async-start | bytes 524288 | tf_op jit(solution)/shard_map/all_to_all | solution.py:328
  166.7 8.3 %collective-permute-start.31 = (bf16[2,128,256]{2,1,0:T(8,128)(2,1)S(1)}, bf16[2,128,256]{2,1,0:T(8,128)(2,1)S(1)}, u32[]{:S(2)}, u32[]{:S(2)}) collective-permute-start(bf16[2,128,256]{2,1,0:T(8,128)(2,1)S(1)} %slice.82), channel_id=1, source_target_pairs={{0,2},{2,4},{4,6},{6,8},{8,10},{10,12},{12,14},{14,0},{1,3},{3,5},... | collective-permute-start | bytes 393224 | tf_op jit(solution)/shard_map/ppermute | solution.py:20
  171.2 6.3 %collective-permute-start.32 = (bf16[2,128,256]{2,1,0:T(8,128)(2,1)S(1)}, bf16[2,128,256]{2,1,0:T(8,128)(2,1)S(1)}, u32[]{:S(2)}, u32[]{:S(2)}) collective-permute-start(bf16[2,128,256]{2,1,0:T(8,128)(2,1)S(1)} %slice.83), channel_id=1, source_target_pairs={{0,14},{2,0},{4,2},{6,4},{8,6},{10,8},{12,10},{14,12},{1,15},{3,1}... | collective-permute-start | bytes 393224 | tf_op jit(solution)/shard_map/ppermute | solution.py:20
  177.5 3.4 %copy-start = (bf16[1,1,256,128,128]{4,3,2,1,0:T(8,128)(2,1)S(1)}, bf16[1,1,256,128,128]{4,3,2,1,0:T(8,128)(2,1)}, u32[]{:S(2)}) copy-start(bf16[1,1,256,128,128]{4,3,2,1,0:T(8,128)(2,1)} %param.12) | copy-start | bytes 25165828
  188.2 2.0 copy-start.1
  190.2 51.9 %all-to-all-start.3 = ((bf16[64,128,256]{2,1,0:T(8,128)(2,1)}), bf16[64,128,256]{2,1,0:T(8,128)(2,1)}, u32[]{:S(2)}, u32[]{:S(2)}) async-start(bf16[64,128,256]{2,1,0:T(8,128)(2,1)} %copy-done.1), calls=%async_computation.3 | async-start | bytes 8388608 | tf_op jit(solution)/shard_map/all_to_all | solution.py:318
